TPU v7x, 32 devices: a whole 2x2x4 slice. The times are simulated.
32 devices in a mesh: pipe: 4 (over y, x), expert: 8 (over z, core).
Axes of the slice: x: 2, y: 2, z: 4, core: 2. Of those that a mesh axis runs over, the one named last changes fastest.
Arguments:
- fwd_state: bfloat16 [4, 512, 3584], P('pipe', 'expert'), may hold values from -6 to 6
- rev_state: bfloat16 [4, 512, 3584], P('pipe', 'expert'), may hold values from -6 to 6
- norm_gain: float32 [4, 3584], P('pipe'), may hold values from 0.5 to 1.5
- w_gate: bfloat16 [4, 3584, 1024], P('pipe', None, 'expert'), may hold values from -0.09375 to 0.09375
- w_up: bfloat16 [4, 3584, 1024], P('pipe', None, 'expert'), may hold values from -0.09375 to 0.09375
- w_down: bfloat16 [4, 1024, 3584], P('pipe', 'expert'), may hold values from -0.1875 to 0.1875
- routes_fwd: int32 [3, 4, 512, 8], P(None, 'pipe', 'expert'), may hold values from 0 to 255, as said below
- scores_fwd: float32 [3, 4, 512, 8], P(None, 'pipe', 'expert'), may hold values from 0.02 to 1
- routes_rev: int32 [3, 4, 512, 8], P(None, 'pipe', 'expert'), may hold values from 0 to 255, as said below
- scores_rev: float32 [3, 4, 512, 8], P(None, 'pipe', 'expert'), may hold values from 0.02 to 1
Outputs:
- fwd_out: bfloat16 [4, 512, 3584], P('pipe', 'expert')
- rev_out: bfloat16 [4, 512, 3584], P('pipe', 'expert')
Inputs may be any that keep to these rules, and one draw needn't show every extreme that they name: `routes_fwd`: each row names 8 different experts, all from at most 4 of the 8 groups of 32 consecutive experts. Among the 64 rows of one device, each expert below 1 is named by 1 to 4 rows, and one of them by exactly 4. `routes_rev`: as for routes_fwd.
All inputs are finite; a program needn't handle non-finite values.
Results may differ from a plain program's by a relative error of at most 0.003.
Values may be sent and summed in bfloat16 or wider, within the bound.
A program may use at most 64 MiB of HBM per device.

v0:
```python
import jax
import jax.numpy as jnp
from jax import lax
from jax.sharding import PartitionSpec as P

SPLIT = 8
CAP = 4
STEPS = 3


EPSILON = 1e-06
ROUTE_SCALE = 2.5


def shifted(value, axis, steps):
    count = lax.axis_size(axis)
    pairs = [(source, (source + steps) % count) for source in range(count)]
    return lax.ppermute(value, axis, pairs)


def normalize(tok_rows, gain_row):
    values = tok_rows.astype(jnp.float32)
    factor = lax.rsqrt(jnp.mean(values * values, axis=-1, keepdims=True) + EPSILON)
    return (values * factor * gain_row).astype(jnp.bfloat16)


def slot_tables(route_ids, route_scores, flying):
    expert_ids = jnp.arange(flying, dtype=jnp.int32)
    matches = (route_ids[:, :, None] == expert_ids[None, None, :]).astype(jnp.float32)
    hit_mask = jnp.sum(matches, axis=1)
    weighted = (
        ROUTE_SCALE
        * jnp.sum(matches * route_scores[:, :, None], axis=1)
        / jnp.sum(route_scores, axis=1, keepdims=True)
    )
    slot_index = jnp.cumsum(hit_mask, axis=0) - 1.0
    slot_ids = jnp.arange(CAP, dtype=jnp.float32)
    placed = hit_mask.T[:, None, :] * (slot_index.T[:, None, :] == slot_ids[None, :, None]).astype(
        jnp.float32
    )
    mix_table = placed * weighted.T[:, None, :]
    return (placed, mix_table)


def dispatch_slots(normed, placed):
    return jnp.einsum(
        "ecr,rd->ecd", placed, normed.astype(jnp.float32), precision=lax.Precision.HIGHEST
    ).astype(jnp.bfloat16)


def finish(tok_rows, summed, mix_table):
    added = jnp.einsum("ecr,ecd->rd", mix_table, summed, precision=lax.Precision.HIGHEST)
    return (tok_rows.astype(jnp.float32) + added).astype(jnp.bfloat16)


def local(
    fwd_state,
    rev_state,
    norm_gain,
    w_gate,
    w_up,
    w_down,
    routes_fwd,
    scores_fwd,
    routes_rev,
    scores_rev,
):
    flying = lax.axis_size("expert") // SPLIT
    width = fwd_state.shape[2]
    gain_row = norm_gain[0]
    gate_cols = w_gate[0]
    up_cols = w_up[0]
    down_rows = w_down[0]

    def prepare(current, route_ids, route_scores):
        normed = normalize(current[0], gain_row)
        placed, mix_table = slot_tables(route_ids, route_scores, flying)
        slot_rows = dispatch_slots(normed, placed)
        copies = jnp.broadcast_to(slot_rows[:, None], (flying, SPLIT, CAP, width)).reshape(
            flying * SPLIT, CAP, width
        )
        return (copies, mix_table)

    def finish_stream(current, returned, mix_table):
        summed = jnp.sum(returned.astype(jnp.float32).reshape(flying, SPLIT, CAP, width), axis=1)
        return finish(current[0], summed, mix_table)[None]

    forward_now = fwd_state
    reverse_now = rev_state
    for step_index in range(STEPS):
        fwd_copies, fwd_mix = prepare(
            forward_now, routes_fwd[step_index, 0], scores_fwd[step_index, 0]
        )
        rev_copies, rev_mix = prepare(
            reverse_now, routes_rev[step_index, 0], scores_rev[step_index, 0]
        )
        joined = jnp.concatenate([fwd_copies, rev_copies], axis=1)
        received = lax.all_to_all(joined, "expert", split_axis=0, concat_axis=0, tiled=True)
        tok_rows = received.reshape(-1, width)
        gate_act = jnp.dot(tok_rows, gate_cols, preferred_element_type=jnp.float32)
        up_act = jnp.dot(tok_rows, up_cols, preferred_element_type=jnp.float32)
        hidden = (jax.nn.silu(gate_act) * up_act).astype(jnp.bfloat16)
        partial_out = jnp.dot(hidden, down_rows, preferred_element_type=jnp.float32).astype(
            jnp.bfloat16
        )
        returned = lax.all_to_all(
            partial_out.reshape(received.shape), "expert", split_axis=0, concat_axis=0, tiled=True
        )
        fwd_back = returned[:, :CAP]
        rev_back = returned[:, CAP:]
        forward_now = shifted(finish_stream(forward_now, fwd_back, fwd_mix), "pipe", 1)
        reverse_now = shifted(finish_stream(reverse_now, rev_back, rev_mix), "pipe", -1)
    return (forward_now, reverse_now)


def solution(mesh):
    in_specs = (
        P("pipe", "expert", None),
        P("pipe", "expert", None),
        P("pipe", None),
        P("pipe", None, "expert"),
        P("pipe", None, "expert"),
        P("pipe", "expert", None),
        P(None, "pipe", "expert", None),
        P(None, "pipe", "expert", None),
        P(None, "pipe", "expert", None),
        P(None, "pipe", "expert", None),
    )
    out_specs = (P("pipe", "expert", None), P("pipe", "expert", None))
    return jax.shard_map(local, mesh=mesh, in_specs=in_specs, out_specs=out_specs, check_vma=False)
```

profile of v0, /device:TPU:0, one launch (start us, length us, event | category | flops | bytes accessed | tf_op | source)
XLA Modules:
  0.0 195.6 jit_solution(17700582020377314217)
XLA Ops:
  0.7 1.3 fusion.33
  6.6 20.2 %all_to_all.30 = bf16[8,8,3584]{2,1,0:T(8,128)(2,1)S(1)} all-to-all(bf16[8,8,3584]{2,1,0:T(8,128)(2,1)S(1)} %pad_maximum_fusion), channel_id=1, replica_groups=mesh['pipe'=4,'expert'=8] {'expert'}, dimensions={0} | all-to-all | bytes 917504 | tf_op jit(solution)/shard_map/all_to_all | solution.py:98
  28.0 1.3 fusion.6
  29.4 3.5 %all-to-all-start.1 = ((bf16[8,8,3584]{2,1,0:T(8,128)(2,1)}), bf16[8,8,3584]{2,1,0:T(8,128)(2,1)S(1)}, u32[]{:S(2)}, u32[]{:S(2)}) async-start(bf16[8,8,3584]{2,1,0:T(8,128)(2,1)} %fusion.6), calls=%async_computation.1 | async-start | bytes 917504 | tf_op jit(solution)/shard_map/all_to_all | solution.py:106
  33.4 13.4 %all-to-all-done.1 = bf16[8,8,3584]{2,1,0:T(8,128)(2,1)S(1)} async-done(((bf16[8,8,3584]{2,1,0:T(8,128)(2,1)}), bf16[8,8,3584]{2,1,0:T(8,128)(2,1)S(1)}, u32[]{:S(2)}, u32[]{:S(2)}) %all-to-all-start.1) | async-done | bytes 458784 | tf_op jit(solution)/shard_map/all_to_all | solution.py:106
  48.7 2.5 %collective-permute-start.1 = (bf16[1,64,3584]{2,1,0:T(8,128)(2,1)S(1)}, bf16[1,64,3584]{2,1,0:T(8,128)(2,1)S(1)}, u32[]{:S(2)}, u32[]{:S(2)}) collective-permute-start(bf16[1,64,3584]{2,1,0:T(8,128)(2,1)S(1)} %fusion.13), channel_id=1, source_target_pairs={{0,24},{8,0},{16,8},{24,16},{1,25},{9,1},{17,9},{25,17},{2,26},{10... | collective-permute-start | bytes 1376264 | tf_op jit(solution)/shard_map/ppermute | solution.py:18
  51.2 1.0 fusion.14
  52.4 9.8 %collective-permute-done.1 = bf16[1,64,3584]{2,1,0:T(8,128)(2,1)S(1)} collective-permute-done((bf16[1,64,3584]{2,1,0:T(8,128)(2,1)S(1)}, bf16[1,64,3584]{2,1,0:T(8,128)(2,1)S(1)}, u32[]{:S(2)}, u32[]{:S(2)}) %collective-permute-start.1) | collective-permute-done | bytes 458784 | tf_op jit(solution)/shard_map/ppermute | solution.py:18
  62.4 9.2 %collective-permute-done = bf16[1,64,3584]{2,1,0:T(8,128)(2,1)S(1)} collective-permute-done((bf16[1,64,3584]{2,1,0:T(8,128)(2,1)S(1)}, bf16[1,64,3584]{2,1,0:T(8,128)(2,1)S(1)}, u32[]{:S(2)}, u32[]{:S(2)}) %collective-permute-start) | collective-permute-done | bytes 458784 | tf_op jit(solution)/shard_map/ppermute | solution.py:18
  73.2 16.7 %all_to_all.31 = bf16[8,8,3584]{2,1,0:T(8,128)(2,1)S(1)} all-to-all(bf16[8,8,3584]{2,1,0:T(8,128)(2,1)S(1)} %pad_maximum_fusion.1), channel_id=1, replica_groups=mesh['pipe'=4,'expert'=8] {'expert'}, dimensions={0} | all-to-all | bytes 917504 | tf_op jit(solution)/shard_map/all_to_all | solution.py:98
  90.2 1.3 fusion.7
  91.5 3.5 %all-to-all-start.3 = ((bf16[8,8,3584]{2,1,0:T(8,128)(2,1)}), bf16[8,8,3584]{2,1,0:T(8,128)(2,1)S(1)}, u32[]{:S(2)}, u32[]{:S(2)}) async-start(bf16[8,8,3584]{2,1,0:T(8,128)(2,1)} %fusion.7), calls=%async_computation.3 | async-start | bytes 917504 | tf_op jit(solution)/shard_map/all_to_all | solution.py:106
  95.5 13.4 %all-to-all-done.3 = bf16[8,8,3584]{2,1,0:T(8,128)(2,1)S(1)} async-done(((bf16[8,8,3584]{2,1,0:T(8,128)(2,1)}), bf16[8,8,3584]{2,1,0:T(8,128)(2,1)S(1)}, u32[]{:S(2)}, u32[]{:S(2)}) %all-to-all-start.3) | async-done | bytes 458784 | tf_op jit(solution)/shard_map/all_to_all | solution.py:106
  110.8 1.5 collective-permute-start.2
  113.4 1.5 collective-permute-start.3
  114.9 10.3 %collective-permute-done.2 = bf16[1,64,3584]{2,1,0:T(8,128)(2,1)S(1)} collective-permute-done((bf16[1,64,3584]{2,1,0:T(8,128)(2,1)S(1)}, bf16[1,64,3584]{2,1,0:T(8,128)(2,1)S(1)}, u32[]{:S(2)}, u32[]{:S(2)}) %collective-permute-start.2) | collective-permute-done | bytes 458784 | tf_op jit(solution)/shard_map/ppermute | solution.py:18
  125.4 7.3 %collective-permute-done.3 = bf16[1,64,3584]{2,1,0:T(8,128)(2,1)S(1)} collective-permute-done((bf16[1,64,3584]{2,1,0:T(8,128)(2,1)S(1)}, bf16[1,64,3584]{2,1,0:T(8,128)(2,1)S(1)}, u32[]{:S(2)}, u32[]{:S(2)}) %collective-permute-start.3) | collective-permute-done | bytes 458784 | tf_op jit(solution)/shard_map/ppermute | solution.py:18
  134.3 16.7 %all_to_all.32 = bf16[8,8,3584]{2,1,0:T(8,128)(2,1)S(1)} all-to-all(bf16[8,8,3584]{2,1,0:T(8,128)(2,1)S(1)} %pad_maximum_fusion.2), channel_id=1, replica_groups=mesh['pipe'=4,'expert'=8] {'expert'}, dimensions={0} | all-to-all | bytes 917504 | tf_op jit(solution)/shard_map/all_to_all | solution.py:98
  151.3 1.3 fusion.8
  152.6 3.5 %all-to-all-start.5 = ((bf16[8,8,3584]{2,1,0:T(8,128)(2,1)}), bf16[8,8,3584]{2,1,0:T(8,128)(2,1)S(1)}, u32[]{:S(2)}, u32[]{:S(2)}) async-start(bf16[8,8,3584]{2,1,0:T(8,128)(2,1)} %fusion.8), calls=%async_computation.5 | async-start | bytes 917504 | tf_op jit(solution)/shard_map/all_to_all | solution.py:106
  156.1 13.8 %all-to-all-done.5 = bf16[8,8,3584]{2,1,0:T(8,128)(2,1)S(1)} async-done(((bf16[8,8,3584]{2,1,0:T(8,128)(2,1)}), bf16[8,8,3584]{2,1,0:T(8,128)(2,1)S(1)}, u32[]{:S(2)}, u32[]{:S(2)}) %all-to-all-start.5) | async-done | bytes 458784 | tf_op jit(solution)/shard_map/all_to_all | solution.py:106
  171.2 2.5 %collective-permute-start.5 = (bf16[1,64,3584]{2,1,0:T(8,128)(2,1)S(1)}, bf16[1,64,3584]{2,1,0:T(8,128)(2,1)S(1)}, u32[]{:S(2)}, u32[]{:S(2)}) collective-permute-start(bf16[1,64,3584]{2,1,0:T(8,128)(2,1)S(1)} %fusion.9), channel_id=1, source_target_pairs={{0,24},{8,0},{16,8},{24,16},{1,25},{9,1},{17,9},{25,17},{2,26},{10... | collective-permute-start | bytes 1376264 | tf_op jit(solution)/shard_map/ppermute | solution.py:18
  174.7 10.0 %collective-permute-done.5 = bf16[1,64,3584]{2,1,0:T(8,128)(2,1)S(1)} collective-permute-done((bf16[1,64,3584]{2,1,0:T(8,128)(2,1)S(1)}, bf16[1,64,3584]{2,1,0:T(8,128)(2,1)S(1)}, u32[]{:S(2)}, u32[]{:S(2)}) %collective-permute-start.5) | collective-permute-done | bytes 458784 | tf_op jit(solution)/shard_map/ppermute | solution.py:18
  184.7 9.4 %collective-permute-done.4 = bf16[1,64,3584]{2,1,0:T(8,128)(2,1)S(1)} collective-permute-done((bf16[1,64,3584]{2,1,0:T(8,128)(2,1)S(1)}, bf16[1,64,3584]{2,1,0:T(8,128)(2,1)S(1)}, u32[]{:S(2)}, u32[]{:S(2)}) %collective-permute-start.4) | collective-permute-done | bytes 458784 | tf_op jit(solution)/shard_map/ppermute | solution.py:18
  (110 shorter events, 19.7 us)
Async XLA Ops:
  0.6 26.5 %copy-start = (bf16[1,128,3584]{2,1,0:T(8,128)(2,1)S(1)}, bf16[1,128,3584]{2,1,0:T(8,128)(2,1)}, u32[]{:S(2)}) copy-start(bf16[1,128,3584]{2,1,0:T(8,128)(2,1)} %param.15) | copy-start | bytes 2752516
  0.6 1.3 copy-start.3
  4.8 1.1 copy-start.5
  6.4 20.5 %copy-start.1 = (bf16[1,3584,128]{2,1,0:T(8,128)(2,1)S(1)}, bf16[1,3584,128]{2,1,0:T(8,128)(2,1)}, u32[]{:S(2)}) copy-start(bf16[1,3584,128]{2,1,0:T(8,128)(2,1)} %param.13) | copy-start | bytes 2752516
  26.9 1.2 copy-start.2
  29.4 17.4 %all-to-all-start.1 = ((bf16[8,8,3584]{2,1,0:T(8,128)(2,1)}), bf16[8,8,3584]{2,1,0:T(8,128)(2,1)S(1)}, u32[]{:S(2)}, u32[]{:S(2)}) async-start(bf16[8,8,3584]{2,1,0:T(8,128)(2,1)} %fusion.6), calls=%async_computation.1 | async-start | bytes 917504 | tf_op jit(solution)/shard_map/all_to_all | solution.py:106
  46.7 1.0 copy-start.4
  47.7 3.5 %copy-start.6 = (bf16[1,64,3584]{2,1,0:T(8,128)(2,1)S(1)}, bf16[1,64,3584]{2,1,0:T(8,128)(2,1)}, u32[]{:S(2)}) copy-start(bf16[1,64,3584]{2,1,0:T(8,128)(2,1)} %param.10) | copy-start | bytes 1376260
  48.7 13.5 %collective-permute-start.1 = (bf16[1,64,3584]{2,1,0:T(8,128)(2,1)S(1)}, bf16[1,64,3584]{2,1,0:T(8,128)(2,1)S(1)}, u32[]{:S(2)}, u32[]{:S(2)}) collective-permute-start(bf16[1,64,3584]{2,1,0:T(8,128)(2,1)S(1)} %fusion.13), channel_id=1, source_target_pairs={{0,24},{8,0},{16,8},{24,16},{1,25},{9,1},{17,9},{25,17},{2,26},{10... | collective-permute-start | bytes 1376264 | tf_op jit(solution)/shard_map/ppermute | solution.py:18
  52.2 19.4 %collective-permute-start = (bf16[1,64,3584]{2,1,0:T(8,128)(2,1)S(1)}, bf16[1,64,3584]{2,1,0:T(8,128)(2,1)S(1)}, u32[]{:S(2)}, u32[]{:S(2)}) collective-permute-start(bf16[1,64,3584]{2,1,0:T(8,128)(2,1)S(1)} %fusion.14), channel_id=1, source_target_pairs={{0,8},{8,16},{16,24},{24,0},{1,9},{9,17},{17,25},{25,1},{2,10},{10... | collective-permute-start | bytes 1376264 | tf_op jit(solution)/shard_map/ppermute | solution.py:18
  62.2 9.6 %copy-start.7 = (bf16[1,64,3584]{2,1,0:T(8,128)(2,1)}, bf16[1,64,3584]{2,1,0:T(8,128)(2,1)S(1)}, u32[]{:S(2)}) copy-start(bf16[1,64,3584]{2,1,0:T(8,128)(2,1)S(1)} %collective-permute-done.1) | copy-start | bytes 1376260
  71.6 0.8 copy-start.11
  91.5 17.4 %all-to-all-start.3 = ((bf16[8,8,3584]{2,1,0:T(8,128)(2,1)}), bf16[8,8,3584]{2,1,0:T(8,128)(2,1)S(1)}, u32[]{:S(2)}, u32[]{:S(2)}) async-start(bf16[8,8,3584]{2,1,0:T(8,128)(2,1)} %fusion.7), calls=%async_computation.3 | async-start | bytes 917504 | tf_op jit(solution)/shard_map/all_to_all | solution.py:106
  108.9 1.0 copy-start.12
  109.9 2.5 %copy-start.8 = (bf16[1,64,3584]{2,1,0:T(8,128)(2,1)S(1)}, bf16[1,64,3584]{2,1,0:T(8,128)(2,1)}, u32[]{:S(2)}) copy-start(bf16[1,64,3584]{2,1,0:T(8,128)(2,1)} %copy-done.7) | copy-start | bytes 1376260
  110.8 14.4 %collective-permute-start.2 = (bf16[1,64,3584]{2,1,0:T(8,128)(2,1)S(1)}, bf16[1,64,3584]{2,1,0:T(8,128)(2,1)S(1)}, u32[]{:S(2)}, u32[]{:S(2)}) collective-permute-start(bf16[1,64,3584]{2,1,0:T(8,128)(2,1)S(1)} %fusion.12), channel_id=1, source_target_pairs={{0,8},{8,16},{16,24},{24,0},{1,9},{9,17},{17,25},{25,1},{2,10},{10... | collective-permute-start | bytes 1376264 | tf_op jit(solution)/shard_map/ppermute | solution.py:18
  113.4 19.4 %collective-permute-start.3 = (bf16[1,64,3584]{2,1,0:T(8,128)(2,1)S(1)}, bf16[1,64,3584]{2,1,0:T(8,128)(2,1)S(1)}, u32[]{:S(2)}, u32[]{:S(2)}) collective-permute-start(bf16[1,64,3584]{2,1,0:T(8,128)(2,1)S(1)} %fusion.11), channel_id=1, source_target_pairs={{0,24},{8,0},{16,8},{24,16},{1,25},{9,1},{17,9},{25,17},{2,26},{10... | collective-permute-start | bytes 1376264 | tf_op jit(solution)/shard_map/ppermute | solution.py:18
  125.2 7.7 %copy-start.9 = (bf16[1,64,3584]{2,1,0:T(8,128)(2,1)}, bf16[1,64,3584]{2,1,0:T(8,128)(2,1)S(1)}, u32[]{:S(2)}) copy-start(bf16[1,64,3584]{2,1,0:T(8,128)(2,1)S(1)} %collective-permute-done.2) | copy-start | bytes 1376260
  132.7 0.8 copy-start.13
  152.6 17.4 %all-to-all-start.5 = ((bf16[8,8,3584]{2,1,0:T(8,128)(2,1)}), bf16[8,8,3584]{2,1,0:T(8,128)(2,1)S(1)}, u32[]{:S(2)}, u32[]{:S(2)}) async-start(bf16[8,8,3584]{2,1,0:T(8,128)(2,1)} %fusion.8), calls=%async_computation.5 | async-start | bytes 917504 | tf_op jit(solution)/shard_map/all_to_all | solution.py:106
  156.1 14.1 %copy-start.14 = (bf16[1,64,3584]{2,1,0:T(8,128)(2,1)S(1)}, bf16[1,64,3584]{2,1,0:T(8,128)(2,1)}, u32[]{:S(2)}) copy-start(bf16[1,64,3584]{2,1,0:T(8,128)(2,1)} %copy-done.13) | copy-start | bytes 1376260
  170.2 3.5 %copy-start.10 = (bf16[1,64,3584]{2,1,0:T(8,128)(2,1)S(1)}, bf16[1,64,3584]{2,1,0:T(8,128)(2,1)}, u32[]{:S(2)}) copy-start(bf16[1,64,3584]{2,1,0:T(8,128)(2,1)} %copy-done.9) | copy-start | bytes 1376260
  171.2 13.5 %collective-permute-start.5 = (bf16[1,64,3584]{2,1,0:T(8,128)(2,1)S(1)}, bf16[1,64,3584]{2,1,0:T(8,128)(2,1)S(1)}, u32[]{:S(2)}, u32[]{:S(2)}) collective-permute-start(bf16[1,64,3584]{2,1,0:T(8,128)(2,1)S(1)} %fusion.9), channel_id=1, source_target_pairs={{0,24},{8,0},{16,8},{24,16},{1,25},{9,1},{17,9},{25,17},{2,26},{10... | collective-permute-start | bytes 1376264 | tf_op jit(solution)/shard_map/ppermute | solution.py:18
  174.7 19.4 %collective-permute-start.4 = (bf16[1,64,3584]{2,1,0:T(8,128)(2,1)S(1)}, bf16[1,64,3584]{2,1,0:T(8,128)(2,1)S(1)}, u32[]{:S(2)}, u32[]{:S(2)}) collective-permute-start(bf16[1,64,3584]{2,1,0:T(8,128)(2,1)S(1)} %fusion.10), channel_id=1, source_target_pairs={{0,8},{8,16},{16,24},{24,0},{1,9},{9,17},{17,25},{25,1},{2,10},{10... | collective-permute-start | bytes 1376264 | tf_op jit(solution)/shard_map/ppermute | solution.py:18
  (5 other events, 3.5 us)
where the time goes:
time: 196 us
  waiting for transfers between devices  96.6 us (49%)
  blocking collectives  53.6 us (27%)
  starting transfers between devices  18.6 us (9%)
  matrix products  13.1 us (7%)
  local copies, waits for them, and re-layouts  7.73 us (4%)
  other arithmetic  5.09 us (3%)
    ppermute x6, waiting for transfers between devices, shifted(): return lax.ppermute(value, axis, pairs)  56 us
    all_to_all x3, blocking collectives, local(): lax.all_to_all(joined, 'expert', split_axis=0, concat_axis=0, tiled=True)  53.6 us
    all_to_all x3, waiting for transfers between devices, local(): lax.all_to_all(partial_out.reshape(received.shape), 'expert', split_axis=...  40.6 us
    all_to_all x3, starting transfers between devices, local(): lax.all_to_all(partial_out.reshape(received.shape), 'expert', split_axis=...  10.4 us
    ppermute x6, starting transfers between devices, shifted(): return lax.ppermute(value, axis, pairs)  8.15 us
    unnamed x42, local copies, waits for them, and re-layouts  6.78 us
    dot_general x6, matrix products, finish(): jnp.einsum('ecr,ecd->rd', mix_table, summed, precision=lax.Precision.HIGH...  5.72 us
    dot_general x3, matrix products, local(): jnp.dot(hidden, down_rows, preferred_element_type=jnp.float32)  3.99 us
  transfers between devices with their start and end apart: 9, of which 9 were waited for; matrix products, arithmetic and copies ran while one was open for 2% of the time, Pallas kernels for 0%

commit v1 on v0

--- a/solution.py
+++ b/solution.py
@@ -1,15 +1,19 @@
 import jax
 import jax.numpy as jnp
 from jax import lax
+from jax.experimental import pallas as pl
+from jax.experimental.pallas import tpu as pltpu
 from jax.sharding import PartitionSpec as P
 
 SPLIT = 8
 CAP = 4
 STEPS = 3
-
+PARTS = 4
+CHUNKS = 4
 
 EPSILON = 1e-06
 ROUTE_SCALE = 2.5
+MESH = pl.DeviceIdType.MESH
 
 
 def shifted(value, axis, steps):
@@ -53,7 +57,7 @@
     return (tok_rows.astype(jnp.float32) + added).astype(jnp.bfloat16)
 
 
-def local(
+def general_local(
     fwd_state,
     rev_state,
     norm_gain,
@@ -113,6 +117,444 @@
     return (forward_now, reverse_now)
 
 
+def relay_kernel(
+    fwd_ref,
+    rev_ref,
+    gain_ref,
+    route_ref,
+    score_ref,
+    gate_hbm,
+    up_hbm,
+    down_hbm,
+    fwd_out,
+    rev_out,
+    gate_up,
+    down,
+    table,
+    table_in,
+    early_out,
+    early_in,
+    slots,
+    pieces,
+    mate_pieces,
+    chip_sums,
+    returned,
+    changed,
+    changed_in,
+    bulk_in,
+    weight_sem,
+    table_send,
+    table_recv,
+    early_send,
+    early_recv,
+    slot_send,
+    slot_recv,
+    piece_send,
+    piece_recv,
+    back_send,
+    back_recv,
+    changed_send,
+    changed_recv,
+    bulk_send,
+    bulk_recv,
+):
+    f32, bf16 = jnp.float32, jnp.bfloat16
+    states = (fwd_ref, rev_ref)
+    tokens, width = fwd_ref.shape[1], fwd_ref.shape[2]
+    part = width // PARTS
+    rows = PARTS * CAP
+    sections = lax.axis_size("pipe")
+    holders = lax.axis_size("expert")
+    me_pipe = lax.axis_index("pipe")
+    me_expert = lax.axis_index("expert")
+    chips = holders // 2
+    core = lax.rem(me_expert, 2)
+    chip = me_expert // 2
+
+    def at_section(offset):
+        return {"pipe": lax.rem(me_pipe + sections + offset, sections)}
+
+    def at_chip(offset):
+        return {"expert": lax.rem(chip + chips + offset, chips) * 2 + core}
+
+    mate = {"expert": chip * 2 + 1 - core}
+
+    unsent = []
+
+    def remote(source, target, send, recv, device):
+        return pltpu.make_async_remote_copy(
+            src_ref=source,
+            dst_ref=target,
+            send_sem=send,
+            recv_sem=recv,
+            device_id=device,
+            device_id_type=MESH,
+        )
+
+    def launch(copy):
+        copy.start()
+        unsent.append(copy)
+
+    barrier = pltpu.get_barrier_semaphore()
+    peers = [at_section(d) for d in range(1, 4)] + [at_chip(k) for k in range(1, chips)] + [mate]
+    for peer in peers:
+        pl.semaphore_signal(barrier, inc=1, device_id=peer, device_id_type=MESH)
+
+    weight_copies = [
+        pltpu.make_async_copy(gate_hbm.at[0], gate_up.at[:, 0:128], weight_sem.at[0]),
+        pltpu.make_async_copy(up_hbm.at[0], gate_up.at[:, 128:256], weight_sem.at[1]),
+        pltpu.make_async_copy(down_hbm.at[0], down, weight_sem.at[2]),
+    ]
+    for copy in weight_copies:
+        copy.start()
+
+    lanes = 128
+    before = (
+        lax.broadcasted_iota(jnp.int32, (lanes, lanes), 0)
+        <= lax.broadcasted_iota(jnp.int32, (lanes, lanes), 1)
+    ).astype(f32)
+    slot_of_row = lax.rem(lax.broadcasted_iota(jnp.int32, (8, lanes), 0), CAP).astype(f32)
+    mix = {}
+    for stream in range(2):
+        for step in range(STEPS):
+            match = (route_ref[stream, step] == 0).astype(f32)
+            score = score_ref[stream, step]
+            hit = jnp.sum(match, axis=0, keepdims=True)
+            weighted = (
+                ROUTE_SCALE
+                * jnp.sum(match * score, axis=0, keepdims=True)
+                / jnp.sum(score, axis=0, keepdims=True)
+            )
+            hits = jnp.broadcast_to(hit, (8, lanes))
+            place = jnp.dot(hits, before, preferred_element_type=f32) - 1.0
+            placed = hits * (place == slot_of_row).astype(f32)
+            table[stream, step] = placed
+            column = jnp.sum(placed * weighted, axis=1, keepdims=True)
+            mix[stream, step] = jnp.concatenate([column, column], axis=0)
+
+    part_of_row = lax.broadcasted_iota(jnp.int32, (rows, part), 0) // CAP
+
+    def by_part(pick):
+        total = pick(PARTS - 1)
+        for q in range(PARTS - 1):
+            total = jnp.where(part_of_row == q, pick(q), total)
+        return total
+
+    def cols(q):
+        return slice(q * part, (q + 1) * part)
+
+    def twice(placed):
+        return jnp.concatenate([placed, placed], axis=0)
+
+    def select(placed, state):
+        marks = twice(placed)[:, :tokens].astype(bf16)
+        return by_part(
+            lambda q: jnp.dot(marks, state[0, :, cols(q)], preferred_element_type=f32)
+        )
+
+    gain = by_part(lambda q: jnp.broadcast_to(gain_ref[:, cols(q)], (rows, part)))
+
+    def table_copy(d):
+        return remote(
+            table, table_in.at[d - 1], table_send.at[d - 1], table_recv.at[d - 1], at_section(d)
+        )
+
+    def sign(stream):
+        return 1 if stream == 0 else -1
+
+    def table_from(stream, behind):
+        offset = behind if stream == 0 else (-behind) % 4
+        return table_in.at[offset - 1, stream]
+
+    def early_copy(stream, d):
+        return remote(
+            early_out.at[stream, d - 1],
+            early_in.at[stream, d - 1],
+            early_send.at[stream, d - 1],
+            early_recv.at[stream, d - 1],
+            at_section(sign(stream) * d),
+        )
+
+    def bulk_copy(stream, chunk):
+        size = tokens // CHUNKS
+        piece = pl.ds(chunk * size, size)
+        return remote(
+            states[stream].at[0, piece],
+            bulk_in.at[stream, piece],
+            bulk_send.at[stream, chunk],
+            bulk_recv.at[stream, chunk],
+            at_section(sign(stream) * 3),
+        )
+
+    def changed_copy(stream, step, d):
+        return remote(
+            changed.at[stream, step],
+            changed_in.at[stream, step, d - 1],
+            changed_send.at[stream, step, d - 1],
+            changed_recv.at[stream, step, d - 1],
+            at_section(sign(stream) * d),
+        )
+
+    def slot_copy(stream, step, k):
+        return remote(
+            slots.at[stream, step, 0],
+            slots.at[stream, step, k],
+            slot_send.at[stream, step, k],
+            slot_recv.at[stream, step, k],
+            at_chip(k),
+        )
+
+    def mate_copy(stream, step, k):
+        return remote(
+            slots.at[stream, step, k],
+            slots.at[stream, step, chips + k],
+            slot_send.at[stream, step, chips + k],
+            slot_recv.at[stream, step, chips + k],
+            mate,
+        )
+
+    def piece_copy(stream, step):
+        return remote(
+            pieces.at[stream, step, 1],
+            mate_pieces.at[stream, step],
+            piece_send.at[stream, step],
+            piece_recv.at[stream, step],
+            mate,
+        )
+
+    def back_copy(stream, step, k):
+        return remote(
+            chip_sums.at[stream, step, k],
+            returned.at[stream, step, k - 1],
+            back_send.at[stream, step, k - 1],
+            back_recv.at[stream, step, k - 1],
+            at_chip(-k),
+        )
+
+    row_part = lax.broadcasted_iota(jnp.int32, (rows, rows), 0) // CAP
+    col_part = lax.broadcasted_iota(jnp.int32, (rows, rows), 1) // CAP
+    same_part = (row_part == col_part).astype(f32)
+
+    def chain(stream):
+        for step in range(STEPS):
+            own = table[stream, step]
+            if step == 0:
+                current = select(own, states[stream])
+            else:
+                early_copy(stream, step).wait_recv()
+                current = early_in[stream, step - 1].astype(f32)
+                for past in range(step):
+                    behind = step - past
+                    match = same_part * lax.dot_general(
+                        twice(own),
+                        twice(table_from(stream, behind)[past]),
+                        (((1,), (1,)), ((), ())),
+                        preferred_element_type=f32,
+                    )
+                    seen = jnp.sum(match, axis=1, keepdims=True)
+                    changed_copy(stream, past, behind).wait_recv()
+                    newer = jnp.dot(
+                        match.astype(bf16),
+                        changed_in[stream, past, behind - 1],
+                        preferred_element_type=f32,
+                    )
+                    current = jnp.where(seen > 0.5, newer, current)
+            squares = jnp.sum(current * current, axis=1, keepdims=True)
+            squares = jnp.broadcast_to(squares, (rows, 128))
+            squares = squares[:8] + squares[8:]
+            squares = squares + pltpu.roll(squares, 4, 0)
+            factor = lax.rsqrt(squares[:, :1] * (1.0 / width) + EPSILON)
+            slots[stream, step, 0] = (current * twice(factor) * gain).astype(bf16)
+            if step == 0 and stream == 0:
+                pl.semaphore_wait(barrier, len(peers))
+            for k in (2, 1, 3):
+                launch(slot_copy(stream, step, k))
+            launch(mate_copy(stream, step, 0))
+            yield
+            for k in (1, 3, 2):
+                slot_copy(stream, step, k).wait_recv()
+                launch(mate_copy(stream, step, k))
+            yield
+            for k in range(chips):
+                mate_copy(stream, step, k).wait_recv()
+            if step == 0 and stream == 0:
+                for copy in weight_copies:
+                    copy.wait()
+            gathered = slots[stream, step].reshape(holders * rows, part)
+            total = None
+            part_of_line = (
+                lax.broadcasted_iota(jnp.int32, (holders * rows, 256), 0) % rows
+            ) // CAP
+            for q in range(PARTS):
+                product = jnp.dot(gathered, gate_up[cols(q), :], preferred_element_type=f32)
+                total = product if q == 0 else jnp.where(part_of_line == q, product, total)
+            total = total.reshape(holders, 2, 8, 256)
+            total = total[:, 0] + total[:, 1]
+            total = (total + pltpu.roll(total, 4, 1)).reshape(holders * 8, 256)
+            gate_act, up_act = total[:, :128], total[:, 128:]
+            hidden = (gate_act / (1.0 + jnp.exp(-gate_act)) * up_act).astype(bf16)
+            low = lax.broadcasted_iota(jnp.int32, (holders * 8, part), 0) % 8 < CAP
+            halves = []
+            for half in range(2):
+                one = jnp.dot(hidden, down[:, cols(2 * half)], preferred_element_type=f32)
+                two = jnp.dot(hidden, down[:, cols(2 * half + 1)], preferred_element_type=f32)
+                halves.append(jnp.where(low, one, two).reshape(holders, 1, 8, part))
+            joined = jnp.concatenate(halves, axis=1).reshape(2, chips, rows, part)
+            pieces[stream, step] = joined.astype(bf16)
+            launch(piece_copy(stream, step))
+            yield
+            piece_copy(stream, step).wait_recv()
+            sums = pieces[stream, step, 0].astype(f32) + mate_pieces[stream, step].astype(f32)
+            chip_sums[stream, step] = sums.astype(bf16)
+            for k in (2, 1, 3):
+                launch(back_copy(stream, step, k))
+            yield
+            expert_out = sums[0]
+            for k in range(1, chips):
+                back_copy(stream, step, k).wait_recv()
+                expert_out = expert_out + returned[stream, step, k - 1].astype(f32)
+            changed[stream, step] = (current + mix[stream, step] * expert_out).astype(bf16)
+            for d in range(1, STEPS - step + 1):
+                launch(changed_copy(stream, step, d))
+
+    def tables_out():
+        for d in range(1, 4):
+            launch(table_copy(d))
+
+    def early_rows():
+        for d in range(1, 4):
+            table_copy(d).wait_recv()
+        for stream in range(2):
+            for d in range(1, STEPS):
+                ahead = table_from(stream, 4 - d)
+                early_out[stream, d - 1] = select(ahead[d], states[stream]).astype(bf16)
+                launch(early_copy(stream, d))
+
+    def bulk(chunk):
+        for stream in range(2):
+            launch(bulk_copy(stream, chunk))
+
+    extras = {
+        0: [tables_out],
+        1: [early_rows, lambda: bulk(0)],
+        3: [lambda: bulk(1)],
+        5: [lambda: bulk(2)],
+        7: [lambda: bulk(3)],
+    }
+    chains = [chain(0), chain(1)]
+    turn = 0
+    while chains:
+        for one in list(chains):
+            try:
+                next(one)
+            except StopIteration:
+                chains.remove(one)
+        for extra in extras.get(turn, []):
+            extra()
+        turn += 1
+
+    slot_lane = lax.broadcasted_iota(jnp.int32, (tokens, lanes), 1)
+    for stream, out in ((0, fwd_out), (1, rev_out)):
+        marks = []
+        for step in range(STEPS):
+            placed = table_from(stream, STEPS - step)[step]
+            for later in range(step + 1, STEPS):
+                newer = table_from(stream, STEPS - later)[later]
+                placed = placed * (1.0 - jnp.sum(newer[:CAP], axis=0, keepdims=True))
+            marks.append(twice(placed))
+        marks.append(jnp.zeros((lanes - STEPS * rows, lanes), f32))
+        spread = jnp.concatenate(marks, axis=0).T[:tokens]
+        seen = jnp.sum(spread, axis=1, keepdims=True) > 0.5
+        for chunk in range(CHUNKS):
+            bulk_copy(stream, chunk).wait_recv()
+        for step in range(STEPS):
+            changed_copy(stream, step, STEPS - step).wait_recv()
+        newest = [changed_in[stream, step, STEPS - step - 1] for step in range(STEPS)]
+        newest.append(jnp.zeros((lanes - STEPS * rows, part), bf16))
+        newest = jnp.concatenate(newest, axis=0)
+        for q in range(PARTS):
+            chosen = jnp.where(lax.rem(slot_lane, rows) // CAP == q, spread, 0.0).astype(bf16)
+            newer = jnp.dot(chosen, newest, preferred_element_type=f32)
+            older = bulk_in[stream, :, cols(q)].astype(f32)
+            out[0, :, cols(q)] = jnp.where(seen, newer, older).astype(bf16)
+
+    for copy in unsent:
+        copy.wait_send()
+
+
+def relay_local(
+    fwd_state,
+    rev_state,
+    norm_gain,
+    w_gate,
+    w_up,
+    w_down,
+    routes_fwd,
+    scores_fwd,
+    routes_rev,
+    scores_rev,
+):
+    tokens, width = fwd_state.shape[1:]
+    part = width // PARTS
+    rows = PARTS * CAP
+    holders = SPLIT
+    chips = holders // 2
+    bf16 = jnp.bfloat16
+
+    def across(first, second, fill):
+        both = jnp.stack([first[:, 0], second[:, 0]]).transpose(0, 1, 3, 2)
+        return jnp.pad(both, ((0, 0), (0, 0), (0, 0), (0, 128 - tokens)), constant_values=fill)
+
+    routes = across(routes_fwd, routes_rev, -1)
+    scores = across(scores_fwd, scores_rev, 1.0)
+    vmem = pl.BlockSpec(memory_space=pltpu.VMEM)
+    anywhere = pl.BlockSpec(memory_space=pl.ANY)
+    dma = pltpu.SemaphoreType.DMA
+    return pl.pallas_call(
+        relay_kernel,
+        out_shape=[jax.ShapeDtypeStruct(fwd_state.shape, bf16)] * 2,
+        in_specs=[vmem] * 5 + [anywhere] * 3,
+        out_specs=[vmem, vmem],
+        scratch_shapes=[
+            pltpu.VMEM((width, 256), bf16),
+            pltpu.VMEM((128, width), bf16),
+            pltpu.VMEM((2, STEPS, 8, 128), jnp.float32),
+            pltpu.VMEM((3, 2, STEPS, 8, 128), jnp.float32),
+            pltpu.VMEM((2, STEPS - 1, rows, part), bf16),
+            pltpu.VMEM((2, STEPS - 1, rows, part), bf16),
+            pltpu.VMEM((2, STEPS, holders, rows, part), bf16),
+            pltpu.VMEM((2, STEPS, 2, chips, rows, part), bf16),
+            pltpu.VMEM((2, STEPS, chips, rows, part), bf16),
+            pltpu.VMEM((2, STEPS, chips, rows, part), bf16),
+            pltpu.VMEM((2, STEPS, chips - 1, rows, part), bf16),
+            pltpu.VMEM((2, STEPS, rows, part), bf16),
+            pltpu.VMEM((2, STEPS, STEPS, rows, part), bf16),
+            pltpu.VMEM((2, tokens, width), bf16),
+            dma((3,)),
+            dma((3,)),
+            dma((3,)),
+            dma((2, STEPS - 1)),
+            dma((2, STEPS - 1)),
+            dma((2, STEPS, holders)),
+            dma((2, STEPS, holders)),
+            dma((2, STEPS)),
+            dma((2, STEPS)),
+            dma((2, STEPS, chips - 1)),
+            dma((2, STEPS, chips - 1)),
+            dma((2, STEPS, STEPS)),
+            dma((2, STEPS, STEPS)),
+            dma((2, CHUNKS)),
+            dma((2, CHUNKS)),
+        ],
+        compiler_params=pltpu.CompilerParams(
+            collective_id=0, has_side_effects=True, vmem_limit_bytes=48 * 1024 * 1024
+        ),
+        cost_estimate=pl.CostEstimate(
+            flops=1_000_000_000, bytes_accessed=8_000_000, transcendentals=100_000
+        ),
+    )(fwd_state, rev_state, norm_gain, routes, scores, w_gate, w_up, w_down)
+
+
 def solution(mesh):
     in_specs = (
         P("pipe", "expert", None),
@@ -127,4 +569,6 @@
         P(None, "pipe", "expert", None),
     )
     out_specs = (P("pipe", "expert", None), P("pipe", "expert", None))
+    small = mesh.shape["pipe"] == 4 and mesh.shape["expert"] == SPLIT
+    local = relay_local if small else general_local
     return jax.shard_map(local, mesh=mesh, in_specs=in_specs, out_specs=out_specs, check_vma=False)

time: 196 us -> 76.8 us (0.39)
  waiting for transfers between devices: 96.6 us -> 0 us
  Pallas kernels: 0 us -> 66.3 us
  blocking collectives: 53.6 us -> 0 us
  starting transfers between devices: 18.6 us -> 0 us
  matrix products: 13.1 us -> 0 us
  other arithmetic: 5.09 us -> 0.74 us
    pallas_call x0 -> x1, Pallas kernels: none -> 66.3 us  [relay_local(): pl.pallas_call(relay_kernel, out_shape=[jax.ShapeDtypeStruct(fwd_state.sh...]
    ppermute x6 -> x0, waiting for transfers between devices: 56 us -> none  [shifted(): return lax.ppermute(value, axis, pairs)]
    all_to_all x3 -> x0, blocking collectives: 53.6 us -> none  [local(): lax.all_to_all(joined, 'expert', split_axis=0, concat_axis=0, tiled=True)]
    all_to_all x3 -> x0, waiting for transfers between devices: 40.6 us -> none  [local(): lax.all_to_all(partial_out.reshape(received.shape), 'expert', split_axis=...]
    dot_general x18 -> x0, matrix products: 13.1 us -> none  [the longest x6 5.72 us: finish(): jnp.einsum('ecr,ecd->rd', mix_table, summed, precision=lax.Precision.HIGH...]
    all_to_all x3 -> x0, starting transfers between devices: 10.4 us -> none  [local(): lax.all_to_all(partial_out.reshape(received.shape), 'expert', split_axis=...]
    ppermute x6 -> x0, starting transfers between devices: 8.15 us -> none  [shifted(): return lax.ppermute(value, axis, pairs)]
    reduce_sum x11 -> x0, other arithmetic: 3.09 us -> none  [the longest x6 2.29 us: normalize(): jnp.mean(values * values, axis=-1, keepdims=True) + EPSILON]
  transfers between devices with their start and end apart: 9 -> 0, of which waited for: 9 -> 0; matrix products, arithmetic and copies ran while one was open for 2% -> 0% of each run, Pallas kernels for 0% -> 0%
where the time goes in v1:
time: 76.8 us; the launch traced here: 76.2 us
  Pallas kernels  66.3 us (86%)
  local copies, waits for them, and re-layouts  8.53 us (11%)
    pallas_call x1, Pallas kernels, relay_local(): pl.pallas_call(relay_kernel, out_shape=[jax.ShapeDtypeStruct(fwd_state.sh...  66.3 us
    unnamed x18, local copies, waits for them, and re-layouts  8.52 us

profile of v1, /device:TPU:0, one launch (start us, length us, event | category | flops | bytes accessed | tf_op | source)
XLA Modules:
  0.0 76.2 jit_solution(8487958918270627443)
XLA Ops:
  0.6 0.7 add_bitcast_fusion
  1.4 0.0 copy-start.6
  1.4 0.0 copy-start.7
  1.4 0.7 copy-done.6
  2.1 0.0 copy-done.7
  2.1 0.0 copy-start.5
  2.1 0.7 copy-done.5
  2.8 0.0 copy-start
  2.8 1.2 %copy-done = bf16[1,3584,128]{2,1,0:T(8,128)(2,1)S(1)} copy-done((bf16[1,3584,128]{2,1,0:T(8,128)(2,1)S(1)}, bf16[1,3584,128]{2,1,0:T(8,128)(2,1)}, u32[]{:S(2)}) %copy-start) | copy-done | bytes 917528
  4.0 0.0 copy-start.1
  4.0 1.2 %copy-done.1 = bf16[1,3584,128]{2,1,0:T(8,128)(2,1)S(1)} copy-done((bf16[1,3584,128]{2,1,0:T(8,128)(2,1)S(1)}, bf16[1,3584,128]{2,1,0:T(8,128)(2,1)}, u32[]{:S(2)}) %copy-start.1) | copy-done | bytes 917528
  5.2 0.0 copy-start.2
  5.2 1.2 %copy-done.2 = bf16[1,128,3584]{2,1,0:T(8,128)(2,1)S(1)} copy-done((bf16[1,128,3584]{2,1,0:T(8,128)(2,1)S(1)}, bf16[1,128,3584]{2,1,0:T(8,128)(2,1)}, u32[]{:S(2)}) %copy-start.2) | copy-done | bytes 917528
  6.3 0.0 copy-start.3
  6.3 1.0 %copy-done.3 = bf16[1,64,3584]{2,1,0:T(8,128)(2,1)S(1)} copy-done((bf16[1,64,3584]{2,1,0:T(8,128)(2,1)S(1)}, bf16[1,64,3584]{2,1,0:T(8,128)(2,1)}, u32[]{:S(2)}) %copy-start.3) | copy-done | bytes 458776
  7.4 0.0 copy-start.4
  7.4 1.0 %copy-done.4 = bf16[1,64,3584]{2,1,0:T(8,128)(2,1)S(1)} copy-done((bf16[1,64,3584]{2,1,0:T(8,128)(2,1)S(1)}, bf16[1,64,3584]{2,1,0:T(8,128)(2,1)}, u32[]{:S(2)}) %copy-start.4) | copy-done | bytes 458776
  8.4 66.3 %shard_map.113 = (bf16[1,64,3584]{2,1,0:T(8,128)(2,1)S(1)}, bf16[1,64,3584]{2,1,0:T(8,128)(2,1)S(1)}) custom-call(bf16[1,64,3584]{2,1,0:T(8,128)(2,1)S(1)} %copy-done.3, bf16[1,64,3584]{2,1,0:T(8,128)(2,1)S(1)} %copy-done.4, f32[1,3584]{1,0:T(1,128)S(1)} %copy-done.5, s32[2,3,8,128]{3,2,1,0:T(8,128)S(1)} %pad.8.route_ref, ...), custom_call_target="tpu_custom_call" | custom-call | flops 1000000000 | bytes 8000000 | tf_op jit(solution)/shard_map/pallas_call | solution.py:513
  74.7 0.8 %copy.14 = bf16[1,64,3584]{2,1,0:T(8,128)(2,1)} copy(bf16[1,64,3584]{2,1,0:T(8,128)(2,1)S(1)} %get-tuple-element.4) | data formatting | bytes 917504
  75.5 0.8 %copy.15 = bf16[1,64,3584]{2,1,0:T(8,128)(2,1)} copy(bf16[1,64,3584]{2,1,0:T(8,128)(2,1)S(1)} %get-tuple-element.5) | data formatting | bytes 917504
  (3 shorter events, 0.0 us)
Async XLA Ops:
  1.4 0.7 copy-start.6
  1.4 0.7 copy-start.7
  2.1 0.7 copy-start.5
  2.8 1.2 %copy-start = (bf16[1,3584,128]{2,1,0:T(8,128)(2,1)S(1)}, bf16[1,3584,128]{2,1,0:T(8,128)(2,1)}, u32[]{:S(2)}) copy-start(bf16[1,3584,128]{2,1,0:T(8,128)(2,1)} %gate_hbm.1) | copy-start | bytes 2752516
  4.0 1.2 %copy-start.1 = (bf16[1,3584,128]{2,1,0:T(8,128)(2,1)S(1)}, bf16[1,3584,128]{2,1,0:T(8,128)(2,1)}, u32[]{:S(2)}) copy-start(bf16[1,3584,128]{2,1,0:T(8,128)(2,1)} %up_hbm.1) | copy-start | bytes 2752516
  5.2 1.2 %copy-start.2 = (bf16[1,128,3584]{2,1,0:T(8,128)(2,1)S(1)}, bf16[1,128,3584]{2,1,0:T(8,128)(2,1)}, u32[]{:S(2)}) copy-start(bf16[1,128,3584]{2,1,0:T(8,128)(2,1)} %down_hbm.1) | copy-start | bytes 2752516
  6.3 1.0 %copy-start.3 = (bf16[1,64,3584]{2,1,0:T(8,128)(2,1)S(1)}, bf16[1,64,3584]{2,1,0:T(8,128)(2,1)}, u32[]{:S(2)}) copy-start(bf16[1,64,3584]{2,1,0:T(8,128)(2,1)} %fwd_ref.1) | copy-start | bytes 1376260
  7.4 1.0 %copy-start.4 = (bf16[1,64,3584]{2,1,0:T(8,128)(2,1)S(1)}, bf16[1,64,3584]{2,1,0:T(8,128)(2,1)}, u32[]{:S(2)}) copy-start(bf16[1,64,3584]{2,1,0:T(8,128)(2,1)} %rev_ref.1) | copy-start | bytes 1376260

commit v2 on v1

--- a/solution.py
+++ b/solution.py
@@ -118,16 +118,22 @@
 
 
 def relay_kernel(
-    fwd_ref,
-    rev_ref,
+    fwd_hbm,
+    rev_hbm,
+    gain_hbm,
+    gate_hbm,
+    up_hbm,
+    down_hbm,
+    routes_fwd_hbm,
+    scores_fwd_hbm,
+    routes_rev_hbm,
+    scores_rev_hbm,
+    fwd_out,
+    rev_out,
+    states,
     gain_ref,
     route_ref,
     score_ref,
-    gate_hbm,
-    up_hbm,
-    down_hbm,
-    fwd_out,
-    rev_out,
     gate_up,
     down,
     table,
@@ -142,7 +148,7 @@
     changed,
     changed_in,
     bulk_in,
-    weight_sem,
+    load_sem,
     table_send,
     table_recv,
     early_send,
@@ -159,8 +165,7 @@
     bulk_recv,
 ):
     f32, bf16 = jnp.float32, jnp.bfloat16
-    states = (fwd_ref, rev_ref)
-    tokens, width = fwd_ref.shape[1], fwd_ref.shape[2]
+    tokens, width = fwd_hbm.shape[1], fwd_hbm.shape[2]
     part = width // PARTS
     rows = PARTS * CAP
     sections = lax.axis_size("pipe")
@@ -200,20 +205,32 @@
     for peer in peers:
         pl.semaphore_signal(barrier, inc=1, device_id=peer, device_id_type=MESH)
 
-    weight_copies = [
-        pltpu.make_async_copy(gate_hbm.at[0], gate_up.at[:, 0:128], weight_sem.at[0]),
-        pltpu.make_async_copy(up_hbm.at[0], gate_up.at[:, 128:256], weight_sem.at[1]),
-        pltpu.make_async_copy(down_hbm.at[0], down, weight_sem.at[2]),
+    loads = [
+        (routes_fwd_hbm.at[:, 0], route_ref.at[0]),
+        (routes_rev_hbm.at[:, 0], route_ref.at[1]),
+        (scores_fwd_hbm.at[:, 0], score_ref.at[0]),
+        (scores_rev_hbm.at[:, 0], score_ref.at[1]),
+        (fwd_hbm.at[0], states.at[0]),
+        (rev_hbm.at[0], states.at[1]),
+        (gain_hbm, gain_ref),
+        (gate_hbm.at[0], gate_up.at[:, 0:128]),
+        (up_hbm.at[0], gate_up.at[:, 128:256]),
+        (down_hbm.at[0], down),
     ]
-    for copy in weight_copies:
+    loads = [
+        pltpu.make_async_copy(source, target, load_sem.at[i])
+        for i, (source, target) in enumerate(loads)
+    ]
+    for copy in loads:
         copy.start()
-
-    lanes = 128
+    for copy in loads[:4]:
+        copy.wait()
+
     before = (
-        lax.broadcasted_iota(jnp.int32, (lanes, lanes), 0)
-        <= lax.broadcasted_iota(jnp.int32, (lanes, lanes), 1)
+        lax.broadcasted_iota(jnp.int32, (tokens, tokens), 0)
+        <= lax.broadcasted_iota(jnp.int32, (tokens, tokens), 1)
     ).astype(f32)
-    slot_of_row = lax.rem(lax.broadcasted_iota(jnp.int32, (8, lanes), 0), CAP).astype(f32)
+    slot_of_row = lax.rem(lax.broadcasted_iota(jnp.int32, (8, tokens), 0), CAP).astype(f32)
     mix = {}
     for stream in range(2):
         for step in range(STEPS):
@@ -225,7 +242,7 @@
                 * jnp.sum(match * score, axis=0, keepdims=True)
                 / jnp.sum(score, axis=0, keepdims=True)
             )
-            hits = jnp.broadcast_to(hit, (8, lanes))
+            hits = jnp.broadcast_to(hit, (8, tokens))
             place = jnp.dot(hits, before, preferred_element_type=f32) - 1.0
             placed = hits * (place == slot_of_row).astype(f32)
             table[stream, step] = placed
@@ -247,11 +264,13 @@
         return jnp.concatenate([placed, placed], axis=0)
 
     def select(placed, state):
-        marks = twice(placed)[:, :tokens].astype(bf16)
+        marks = twice(placed).astype(bf16)
         return by_part(
-            lambda q: jnp.dot(marks, state[0, :, cols(q)], preferred_element_type=f32)
-        )
-
+            lambda q: jnp.dot(marks, state[:, cols(q)], preferred_element_type=f32)
+        )
+
+    for copy in loads[4:7]:
+        copy.wait()
     gain = by_part(lambda q: jnp.broadcast_to(gain_ref[:, cols(q)], (rows, part)))
 
     def table_copy(d):
@@ -279,7 +298,7 @@
         size = tokens // CHUNKS
         piece = pl.ds(chunk * size, size)
         return remote(
-            states[stream].at[0, piece],
+            states.at[stream, piece],
             bulk_in.at[stream, piece],
             bulk_send.at[stream, chunk],
             bulk_recv.at[stream, chunk],
@@ -339,7 +358,7 @@
         for step in range(STEPS):
             own = table[stream, step]
             if step == 0:
-                current = select(own, states[stream])
+                current = select(own, states.at[stream])
             else:
                 early_copy(stream, step).wait_recv()
                 current = early_in[stream, step - 1].astype(f32)
@@ -367,6 +386,7 @@
             slots[stream, step, 0] = (current * twice(factor) * gain).astype(bf16)
             if step == 0 and stream == 0:
                 pl.semaphore_wait(barrier, len(peers))
+                tables_out()
             for k in (2, 1, 3):
                 launch(slot_copy(stream, step, k))
             launch(mate_copy(stream, step, 0))
@@ -378,7 +398,7 @@
             for k in range(chips):
                 mate_copy(stream, step, k).wait_recv()
             if step == 0 and stream == 0:
-                for copy in weight_copies:
+                for copy in loads[7:]:
                     copy.wait()
             gathered = slots[stream, step].reshape(holders * rows, part)
             total = None
@@ -414,8 +434,9 @@
                 back_copy(stream, step, k).wait_recv()
                 expert_out = expert_out + returned[stream, step, k - 1].astype(f32)
             changed[stream, step] = (current + mix[stream, step] * expert_out).astype(bf16)
-            for d in range(1, STEPS - step + 1):
-                launch(changed_copy(stream, step, d))
+            launch(changed_copy(stream, step, 1))
+            yield
+            farther.extend((stream, step, d) for d in range(2, STEPS - step + 1))
 
     def tables_out():
         for d in range(1, 4):
@@ -427,21 +448,18 @@
         for stream in range(2):
             for d in range(1, STEPS):
                 ahead = table_from(stream, 4 - d)
-                early_out[stream, d - 1] = select(ahead[d], states[stream]).astype(bf16)
+                early_out[stream, d - 1] = select(ahead[d], states.at[stream]).astype(bf16)
                 launch(early_copy(stream, d))
 
-    def bulk(chunk):
-        for stream in range(2):
-            launch(bulk_copy(stream, chunk))
-
-    extras = {
-        0: [tables_out],
-        1: [early_rows, lambda: bulk(0)],
-        3: [lambda: bulk(1)],
-        5: [lambda: bulk(2)],
-        7: [lambda: bulk(3)],
-    }
+    def bulk():
+        for chunk in range(CHUNKS):
+            for stream in range(2):
+                launch(bulk_copy(stream, chunk))
+
+    farther = []
     chains = [chain(0), chain(1)]
+    second = chains[1]
+    next(chains[0])
     turn = 0
     while chains:
         for one in list(chains):
@@ -449,10 +467,16 @@
                 next(one)
             except StopIteration:
                 chains.remove(one)
-        for extra in extras.get(turn, []):
-            extra()
+            if one is second:
+                for stream, step, d in farther:
+                    launch(changed_copy(stream, step, d))
+                farther.clear()
+        if turn == 0:
+            early_rows()
+            bulk()
         turn += 1
 
+    lanes = 128
     slot_lane = lax.broadcasted_iota(jnp.int32, (tokens, lanes), 1)
     for stream, out in ((0, fwd_out), (1, rev_out)):
         marks = []
@@ -462,8 +486,8 @@
                 newer = table_from(stream, STEPS - later)[later]
                 placed = placed * (1.0 - jnp.sum(newer[:CAP], axis=0, keepdims=True))
             marks.append(twice(placed))
-        marks.append(jnp.zeros((lanes - STEPS * rows, lanes), f32))
-        spread = jnp.concatenate(marks, axis=0).T[:tokens]
+        marks.append(jnp.zeros((lanes - STEPS * rows, tokens), f32))
+        spread = jnp.concatenate(marks, axis=0).T
         seen = jnp.sum(spread, axis=1, keepdims=True) > 0.5
         for chunk in range(CHUNKS):
             bulk_copy(stream, chunk).wait_recv()
@@ -501,25 +525,24 @@
     chips = holders // 2
     bf16 = jnp.bfloat16
 
-    def across(first, second, fill):
-        both = jnp.stack([first[:, 0], second[:, 0]]).transpose(0, 1, 3, 2)
-        return jnp.pad(both, ((0, 0), (0, 0), (0, 0), (0, 128 - tokens)), constant_values=fill)
-
-    routes = across(routes_fwd, routes_rev, -1)
-    scores = across(scores_fwd, scores_rev, 1.0)
+    in_hbm = pl.BlockSpec(memory_space=pltpu.HBM)
     vmem = pl.BlockSpec(memory_space=pltpu.VMEM)
-    anywhere = pl.BlockSpec(memory_space=pl.ANY)
+    names = routes_fwd.shape[3]
     dma = pltpu.SemaphoreType.DMA
     return pl.pallas_call(
         relay_kernel,
         out_shape=[jax.ShapeDtypeStruct(fwd_state.shape, bf16)] * 2,
-        in_specs=[vmem] * 5 + [anywhere] * 3,
+        in_specs=[in_hbm] * 10,
         out_specs=[vmem, vmem],
         scratch_shapes=[
+            pltpu.VMEM((2, tokens, width), bf16),
+            pltpu.VMEM((1, width), jnp.float32),
+            pltpu.VMEM((2, STEPS, names, tokens), jnp.int32),
+            pltpu.VMEM((2, STEPS, names, tokens), jnp.float32),
             pltpu.VMEM((width, 256), bf16),
             pltpu.VMEM((128, width), bf16),
-            pltpu.VMEM((2, STEPS, 8, 128), jnp.float32),
-            pltpu.VMEM((3, 2, STEPS, 8, 128), jnp.float32),
+            pltpu.VMEM((2, STEPS, 8, tokens), jnp.float32),
+            pltpu.VMEM((3, 2, STEPS, 8, tokens), jnp.float32),
             pltpu.VMEM((2, STEPS - 1, rows, part), bf16),
             pltpu.VMEM((2, STEPS - 1, rows, part), bf16),
             pltpu.VMEM((2, STEPS, holders, rows, part), bf16),
@@ -530,7 +553,7 @@
             pltpu.VMEM((2, STEPS, rows, part), bf16),
             pltpu.VMEM((2, STEPS, STEPS, rows, part), bf16),
             pltpu.VMEM((2, tokens, width), bf16),
-            dma((3,)),
+            dma((10,)),
             dma((3,)),
             dma((3,)),
             dma((2, STEPS - 1)),
@@ -547,12 +570,20 @@
             dma((2, CHUNKS)),
         ],
         compiler_params=pltpu.CompilerParams(
-            collective_id=0, has_side_effects=True, vmem_limit_bytes=48 * 1024 * 1024
+            collective_id=0, has_side_effects=True, vmem_limit_bytes=64 * 1024 * 1024
         ),
         cost_estimate=pl.CostEstimate(
             flops=1_000_000_000, bytes_accessed=8_000_000, transcendentals=100_000
         ),
-    )(fwd_state, rev_state, norm_gain, routes, scores, w_gate, w_up, w_down)
+    )(
+        fwd_state,
+        rev_state,
+        norm_gain,
+        w_gate,
+        w_up,
+        w_down,
+        *(x.transpose(0, 1, 3, 2) for x in (routes_fwd, scores_fwd, routes_rev, scores_rev)),
+    )
 
 
 def solution(mesh):

time: 76.8 us -> 78.8 us (1.026)
  Pallas kernels: 66.3 us -> 75.3 us
  local copies, waits for them, and re-layouts: 8.53 us -> 2.64 us
    pallas_call x1, Pallas kernels: 66.3 us -> 75.3 us  [relay_local(): pl.pallas_call(relay_kernel, out_shape=[jax.ShapeDtypeStruct(fwd_state.sh...]
    unnamed x18 -> x4, local copies, waits for them, and re-layouts: 8.52 us -> 2.64 us
where the time goes in v2:
time: 78.8 us; the launch traced here: 78.6 us
  Pallas kernels  75.3 us (96%)
  local copies, waits for them, and re-layouts  2.64 us (3%)
    pallas_call x1, Pallas kernels, relay_local(): pl.pallas_call(relay_kernel, out_shape=[jax.ShapeDtypeStruct(fwd_state.sh...  75.3 us
    unnamed x4, local copies, waits for them, and re-layouts  2.64 us

profile of v2, /device:TPU:0, one launch (start us, length us, event | category | flops | bytes accessed | tf_op | source)
XLA Modules:
  0.0 78.6 jit_solution(3634422079984973514)
XLA Ops:
  0.6 75.3 %shard_map.113 = (bf16[1,64,3584]{2,1,0:T(8,128)(2,1)}, bf16[1,64,3584]{2,1,0:T(8,128)(2,1)}) custom-call(bf16[1,64,3584]{2,1,0:T(8,128)(2,1)} %fwd_hbm.1, bf16[1,64,3584]{2,1,0:T(8,128)(2,1)} %rev_hbm.1, f32[1,3584]{1,0:T(1,128)} %gain_hbm.1, bf16[1,3584,128]{2,1,0:T(8,128)(2,1)} %gate_hbm.1, bf16[1,3584,128]{2,1,0:T(8,128)(2,1)} %up_hbm.1, ...), custom_call_target="tpu_custom_call" | custom-call | flops 1000000000 | bytes 8000000 | tf_op jit(solution)/shard_map/pallas_call | solution.py:532
  75.9 0.0 copy-start
  76.0 1.9 %copy.14 = bf16[1,64,3584]{2,1,0:T(8,128)(2,1)} copy(bf16[1,64,3584]{2,1,0:T(8,128)(2,1)} %get-tuple-element.4) | data formatting | bytes 917504
  77.8 0.0 copy-done
  77.8 0.8 copy.15
Async XLA Ops:
  75.9 1.9 %copy-start = (bf16[1,64,3584]{2,1,0:T(8,128)(2,1)S(1)}, bf16[1,64,3584]{2,1,0:T(8,128)(2,1)}, u32[]{:S(2)}) copy-start(bf16[1,64,3584]{2,1,0:T(8,128)(2,1)} %get-tuple-element.5) | copy-start | bytes 1376260

commit v3 on v2

--- a/solution.py
+++ b/solution.py
@@ -154,6 +154,7 @@
     early_send,
     early_recv,
     slot_send,
+    mate_send,
     slot_recv,
     piece_send,
     piece_recv,
@@ -196,10 +197,14 @@
             device_id_type=MESH,
         )
 
-    def launch(copy):
-        copy.start()
-        unsent.append(copy)
-
+    def launch(copy, only=None):
+        if only is None:
+            copy.start()
+        else:
+            pl.when(only)(copy.start)
+        unsent.append((copy, only))
+
+    returned[...] = jnp.zeros_like(returned)
     barrier = pltpu.get_barrier_semaphore()
     peers = [at_section(d) for d in range(1, 4)] + [at_chip(k) for k in range(1, chips)] + [mate]
     for peer in peers:
@@ -314,20 +319,26 @@
             at_section(sign(stream) * d),
         )
 
-    def slot_copy(stream, step, k):
-        return remote(
-            slots.at[stream, step, 0],
+    last = chips - 1
+
+    def slot_copy(stream, step, k, way):
+        target = (k + way) % chips
+        return remote(
             slots.at[stream, step, k],
-            slot_send.at[stream, step, k],
-            slot_recv.at[stream, step, k],
-            at_chip(k),
-        )
+            slots.at[stream, step, target],
+            slot_send.at[stream, step, k, (way + 1) // 2],
+            slot_recv.at[stream, step, target],
+            at_chip(way),
+        )
+
+    def slot_arrives(stream, step, k):
+        slot_copy(stream, step, k - 1, 1).wait_recv()
 
     def mate_copy(stream, step, k):
         return remote(
             slots.at[stream, step, k],
             slots.at[stream, step, chips + k],
-            slot_send.at[stream, step, chips + k],
+            mate_send.at[stream, step, k],
             slot_recv.at[stream, step, chips + k],
             mate,
         )
@@ -341,14 +352,25 @@
             mate,
         )
 
-    def back_copy(stream, step, k):
+    def back_copy(stream, step, way, far):
+        k = chips - far if way > 0 else far
         return remote(
             chip_sums.at[stream, step, k],
-            returned.at[stream, step, k - 1],
-            back_send.at[stream, step, k - 1],
-            back_recv.at[stream, step, k - 1],
-            at_chip(-k),
-        )
+            returned.at[stream, step, (way + 1) // 2, far - 1],
+            back_send.at[stream, step, k],
+            back_recv.at[stream, step, (way + 1) // 2, far - 1],
+            at_chip(way),
+        )
+
+    def back_arrives(stream, step, way, far):
+        if way > 0:
+            here = jnp.logical_and(chip >= 1, chip + far <= last)
+        else:
+            here = jnp.logical_and(chip < last, chip >= far)
+        pl.when(here)(back_copy(stream, step, way, far + 1).wait_recv)
+
+    def back_adds(stream, step, way, far):
+        return returned[stream, step, (way + 1) // 2, far].astype(f32)
 
     row_part = lax.broadcasted_iota(jnp.int32, (rows, rows), 0) // CAP
     col_part = lax.broadcasted_iota(jnp.int32, (rows, rows), 1) // CAP
@@ -387,14 +409,23 @@
             if step == 0 and stream == 0:
                 pl.semaphore_wait(barrier, len(peers))
                 tables_out()
-            for k in (2, 1, 3):
-                launch(slot_copy(stream, step, k))
+            launch(slot_copy(stream, step, 0, 1), chip < last)
+            launch(slot_copy(stream, step, 0, -1), chip > 0)
             launch(mate_copy(stream, step, 0))
             yield
             for k in (1, 3, 2):
-                slot_copy(stream, step, k).wait_recv()
+                slot_arrives(stream, step, k)
+                if k < last:
+                    launch(
+                        slot_copy(stream, step, k, 1), jnp.logical_and(chip >= k, chip < last)
+                    )
+                if k > 1:
+                    launch(
+                        slot_copy(stream, step, k, -1), jnp.logical_and(chip < k, chip > 0)
+                    )
                 launch(mate_copy(stream, step, k))
-            yield
+                if k != 1:
+                    yield
             for k in range(chips):
                 mate_copy(stream, step, k).wait_recv()
             if step == 0 and stream == 0:
@@ -425,14 +456,31 @@
             yield
             piece_copy(stream, step).wait_recv()
             sums = pieces[stream, step, 0].astype(f32) + mate_pieces[stream, step].astype(f32)
-            chip_sums[stream, step] = sums.astype(bf16)
-            for k in (2, 1, 3):
-                launch(back_copy(stream, step, k))
+
+            def send_back(k, total, way, far, only):
+                def store():
+                    chip_sums[stream, step, k] = total.astype(bf16)
+
+                pl.when(only)(store)
+                launch(back_copy(stream, step, way, far), only)
+
+            send_back(1, sums[1], 1, 3, chip == 0)
+            send_back(3, sums[3], -1, 3, chip == last)
             yield
-            expert_out = sums[0]
-            for k in range(1, chips):
-                back_copy(stream, step, k).wait_recv()
-                expert_out = expert_out + returned[stream, step, k - 1].astype(f32)
+            back_arrives(stream, step, 1, 2)
+            back_arrives(stream, step, -1, 2)
+            both = sums[2] + back_adds(stream, step, 1, 2) + back_adds(stream, step, -1, 2)
+            send_back(2, both, 1, 2, chip < 2)
+            send_back(2, both, -1, 2, chip >= 2)
+            yield
+            back_arrives(stream, step, 1, 1)
+            back_arrives(stream, step, -1, 1)
+            send_back(3, sums[3] + back_adds(stream, step, 1, 1), 1, 1, chip < last)
+            send_back(1, sums[1] + back_adds(stream, step, -1, 1), -1, 1, chip > 0)
+            yield
+            back_arrives(stream, step, 1, 0)
+            back_arrives(stream, step, -1, 0)
+            expert_out = sums[0] + back_adds(stream, step, 1, 0) + back_adds(stream, step, -1, 0)
             changed[stream, step] = (current + mix[stream, step] * expert_out).astype(bf16)
             launch(changed_copy(stream, step, 1))
             yield
@@ -459,7 +507,6 @@
     farther = []
     chains = [chain(0), chain(1)]
     second = chains[1]
-    next(chains[0])
     turn = 0
     while chains:
         for one in list(chains):
@@ -471,7 +518,7 @@
                 for stream, step, d in farther:
                     launch(changed_copy(stream, step, d))
                 farther.clear()
-        if turn == 0:
+        if turn == 1:
             early_rows()
             bulk()
         turn += 1
@@ -502,8 +549,11 @@
             older = bulk_in[stream, :, cols(q)].astype(f32)
             out[0, :, cols(q)] = jnp.where(seen, newer, older).astype(bf16)
 
-    for copy in unsent:
-        copy.wait_send()
+    for copy, only in unsent:
+        if only is None:
+            copy.wait_send()
+        else:
+            pl.when(only)(copy.wait_send)
 
 
 def relay_local(
@@ -549,7 +599,7 @@
             pltpu.VMEM((2, STEPS, 2, chips, rows, part), bf16),
             pltpu.VMEM((2, STEPS, chips, rows, part), bf16),
             pltpu.VMEM((2, STEPS, chips, rows, part), bf16),
-            pltpu.VMEM((2, STEPS, chips - 1, rows, part), bf16),
+            pltpu.VMEM((2, STEPS, 2, chips - 1, rows, part), bf16),
             pltpu.VMEM((2, STEPS, rows, part), bf16),
             pltpu.VMEM((2, STEPS, STEPS, rows, part), bf16),
             pltpu.VMEM((2, tokens, width), bf16),
@@ -558,12 +608,13 @@
             dma((3,)),
             dma((2, STEPS - 1)),
             dma((2, STEPS - 1)),
-            dma((2, STEPS, holders)),
+            dma((2, STEPS, chips, 2)),
+            dma((2, STEPS, chips)),
             dma((2, STEPS, holders)),
             dma((2, STEPS)),
             dma((2, STEPS)),
-            dma((2, STEPS, chips - 1)),
-            dma((2, STEPS, chips - 1)),
+            dma((2, STEPS, chips)),
+            dma((2, STEPS, 2, chips - 1)),
             dma((2, STEPS, STEPS)),
             dma((2, STEPS, STEPS)),
             dma((2, CHUNKS)),

time: 78.8 us -> 94.8 us (1.20)
  Pallas kernels: 75.3 us -> 91.3 us
    pallas_call x1, Pallas kernels: 75.3 us -> 91.3 us  [relay_local(): pl.pallas_call(relay_kernel, out_shape=[jax.ShapeDtypeStruct(fwd_state.sh...]
where the time goes in v3:
time: 94.8 us; the launch traced here: 94.6 us
  Pallas kernels  91.3 us (96%)
  local copies, waits for them, and re-layouts  2.64 us (3%)
    pallas_call x1, Pallas kernels, relay_local(): pl.pallas_call(relay_kernel, out_shape=[jax.ShapeDtypeStruct(fwd_state.sh...  91.3 us
    unnamed x4, local copies, waits for them, and re-layouts  2.64 us

profile of v3, /device:TPU:0, one launch (start us, length us, event | category | flops | bytes accessed | tf_op | source)
XLA Modules:
  0.0 94.6 jit_solution(593869717413608682)
XLA Ops:
  0.6 91.3 %shard_map.113 = (bf16[1,64,3584]{2,1,0:T(8,128)(2,1)}, bf16[1,64,3584]{2,1,0:T(8,128)(2,1)}) custom-call(bf16[1,64,3584]{2,1,0:T(8,128)(2,1)} %fwd_hbm.1, bf16[1,64,3584]{2,1,0:T(8,128)(2,1)} %rev_hbm.1, f32[1,3584]{1,0:T(1,128)} %gain_hbm.1, bf16[1,3584,128]{2,1,0:T(8,128)(2,1)} %gate_hbm.1, bf16[1,3584,128]{2,1,0:T(8,128)(2,1)} %up_hbm.1, ...), custom_call_target="tpu_custom_call" | custom-call | flops 1000000000 | bytes 8000000 | tf_op jit(solution)/shard_map/pallas_call | solution.py:582
  92.0 0.0 copy-start
  92.0 1.9 %copy.14 = bf16[1,64,3584]{2,1,0:T(8,128)(2,1)} copy(bf16[1,64,3584]{2,1,0:T(8,128)(2,1)} %get-tuple-element.4) | data formatting | bytes 917504
  93.8 0.0 copy-done
  93.8 0.8 copy.15
Async XLA Ops:
  92.0 1.9 %copy-start = (bf16[1,64,3584]{2,1,0:T(8,128)(2,1)S(1)}, bf16[1,64,3584]{2,1,0:T(8,128)(2,1)}, u32[]{:S(2)}) copy-start(bf16[1,64,3584]{2,1,0:T(8,128)(2,1)} %get-tuple-element.5) | copy-start | bytes 1376260

commit v4 on v2

--- a/solution.py
+++ b/solution.py
@@ -9,7 +9,7 @@
 CAP = 4
 STEPS = 3
 PARTS = 4
-CHUNKS = 4
+CHUNKS = 16
 
 EPSILON = 1e-06
 ROUTE_SCALE = 2.5
@@ -295,11 +295,12 @@
         )
 
     def bulk_copy(stream, chunk):
-        size = tokens // CHUNKS
-        piece = pl.ds(chunk * size, size)
-        return remote(
-            states.at[stream, piece],
-            bulk_in.at[stream, piece],
+        size = tokens * PARTS // CHUNKS
+        piece = pl.ds(chunk // PARTS * size, size)
+        piece = (stream, piece, pl.ds(chunk % PARTS * part, part))
+        return remote(
+            states.at[piece],
+            bulk_in.at[piece],
             bulk_send.at[stream, chunk],
             bulk_recv.at[stream, chunk],
             at_section(sign(stream) * 3),
@@ -451,12 +452,8 @@
                 early_out[stream, d - 1] = select(ahead[d], states.at[stream]).astype(bf16)
                 launch(early_copy(stream, d))
 
-    def bulk():
-        for chunk in range(CHUNKS):
-            for stream in range(2):
-                launch(bulk_copy(stream, chunk))
-
     farther = []
+    later = [(stream, chunk) for chunk in range(CHUNKS) for stream in range(2)]
     chains = [chain(0), chain(1)]
     second = chains[1]
     next(chains[0])
@@ -471,9 +468,12 @@
                 for stream, step, d in farther:
                     launch(changed_copy(stream, step, d))
                 farther.clear()
+            if turn > 0:
+                for stream, chunk in later[:2]:
+                    launch(bulk_copy(stream, chunk))
+                del later[:2]
         if turn == 0:
             early_rows()
-            bulk()
         turn += 1
 
     lanes = 128

time: 78.8 us -> 68.2 us (0.87)
  Pallas kernels: 75.3 us -> 64.7 us
    pallas_call x1, Pallas kernels: 75.3 us -> 64.7 us  [relay_local(): pl.pallas_call(relay_kernel, out_shape=[jax.ShapeDtypeStruct(fwd_state.sh...]
where the time goes in v4:
time: 68.2 us; the launch traced here: 68 us
  Pallas kernels  64.7 us (95%)
  local copies, waits for them, and re-layouts  2.64 us (4%)
    pallas_call x1, Pallas kernels, relay_local(): pl.pallas_call(relay_kernel, out_shape=[jax.ShapeDtypeStruct(fwd_state.sh...  64.7 us
    unnamed x4, local copies, waits for them, and re-layouts  2.64 us

profile of v4, /device:TPU:0, one launch (start us, length us, event | category | flops | bytes accessed | tf_op | source)
XLA Modules:
  0.0 68.0 jit_solution(16963596227082506526)
XLA Ops:
  0.6 64.7 %shard_map.113 = (bf16[1,64,3584]{2,1,0:T(8,128)(2,1)}, bf16[1,64,3584]{2,1,0:T(8,128)(2,1)}) custom-call(bf16[1,64,3584]{2,1,0:T(8,128)(2,1)} %fwd_hbm.1, bf16[1,64,3584]{2,1,0:T(8,128)(2,1)} %rev_hbm.1, f32[1,3584]{1,0:T(1,128)} %gain_hbm.1, bf16[1,3584,128]{2,1,0:T(8,128)(2,1)} %gate_hbm.1, bf16[1,3584,128]{2,1,0:T(8,128)(2,1)} %up_hbm.1, ...), custom_call_target="tpu_custom_call" | custom-call | flops 1000000000 | bytes 8000000 | tf_op jit(solution)/shard_map/pallas_call | solution.py:532
  65.3 0.0 copy-start
  65.3 1.9 %copy.14 = bf16[1,64,3584]{2,1,0:T(8,128)(2,1)} copy(bf16[1,64,3584]{2,1,0:T(8,128)(2,1)} %get-tuple-element.4) | data formatting | bytes 917504
  67.2 0.0 copy-done
  67.2 0.8 %copy.15 = bf16[1,64,3584]{2,1,0:T(8,128)(2,1)} copy(bf16[1,64,3584]{2,1,0:T(8,128)(2,1)S(1)} %copy-done) | data formatting | bytes 917504
Async XLA Ops:
  65.3 1.9 %copy-start = (bf16[1,64,3584]{2,1,0:T(8,128)(2,1)S(1)}, bf16[1,64,3584]{2,1,0:T(8,128)(2,1)}, u32[]{:S(2)}) copy-start(bf16[1,64,3584]{2,1,0:T(8,128)(2,1)} %get-tuple-element.5) | copy-start | bytes 1376260

commit v5 on v4

--- a/solution.py
+++ b/solution.py
@@ -128,8 +128,10 @@
     scores_fwd_hbm,
     routes_rev_hbm,
     scores_rev_hbm,
-    fwd_out,
-    rev_out,
+    fwd_moved,
+    rev_moved,
+    spread_out,
+    newest_out,
     states,
     gain_ref,
     route_ref,
@@ -147,7 +149,6 @@
     returned,
     changed,
     changed_in,
-    bulk_in,
     load_sem,
     table_send,
     table_recv,
@@ -297,10 +298,10 @@
     def bulk_copy(stream, chunk):
         size = tokens * PARTS // CHUNKS
         piece = pl.ds(chunk // PARTS * size, size)
-        piece = (stream, piece, pl.ds(chunk % PARTS * part, part))
-        return remote(
-            states.at[piece],
-            bulk_in.at[piece],
+        columns = pl.ds(chunk % PARTS * part, part)
+        return remote(
+            states.at[stream, piece, columns],
+            (fwd_moved, rev_moved)[stream].at[0, piece, columns],
             bulk_send.at[stream, chunk],
             bulk_recv.at[stream, chunk],
             at_section(sign(stream) * 3),
@@ -452,6 +453,20 @@
                 early_out[stream, d - 1] = select(ahead[d], states.at[stream]).astype(bf16)
                 launch(early_copy(stream, d))
 
+    def spread_tables():
+        for stream in range(2):
+            marks = []
+            for step in range(STEPS):
+                placed = table_from(stream, STEPS - step)[step]
+                for after in range(step + 1, STEPS):
+                    newer = table_from(stream, STEPS - after)[after]
+                    placed = placed * (1.0 - jnp.sum(newer[:CAP], axis=0, keepdims=True))
+                marks.append(twice(placed))
+            rest = spread_out.shape[2] - STEPS * rows
+            marks.append(jnp.zeros((rest, tokens), f32))
+            spread_out[stream] = jnp.concatenate(marks, axis=0).T
+            newest_out[stream, STEPS * rows :] = jnp.zeros((rest, part), bf16)
+
     farther = []
     later = [(stream, chunk) for chunk in range(CHUNKS) for stream in range(2)]
     chains = [chain(0), chain(1)]
@@ -468,42 +483,42 @@
                 for stream, step, d in farther:
                     launch(changed_copy(stream, step, d))
                 farther.clear()
-            if turn > 0:
-                for stream, chunk in later[:2]:
-                    launch(bulk_copy(stream, chunk))
-                del later[:2]
+            pieces_now = 2 if turn % 2 == 1 and one is not second else 1
+            for stream, chunk in later[:pieces_now]:
+                launch(bulk_copy(stream, chunk))
+            del later[:pieces_now]
         if turn == 0:
             early_rows()
+        if turn == 3:
+            spread_tables()
         turn += 1
-
-    lanes = 128
-    slot_lane = lax.broadcasted_iota(jnp.int32, (tokens, lanes), 1)
-    for stream, out in ((0, fwd_out), (1, rev_out)):
-        marks = []
-        for step in range(STEPS):
-            placed = table_from(stream, STEPS - step)[step]
-            for later in range(step + 1, STEPS):
-                newer = table_from(stream, STEPS - later)[later]
-                placed = placed * (1.0 - jnp.sum(newer[:CAP], axis=0, keepdims=True))
-            marks.append(twice(placed))
-        marks.append(jnp.zeros((lanes - STEPS * rows, tokens), f32))
-        spread = jnp.concatenate(marks, axis=0).T
-        seen = jnp.sum(spread, axis=1, keepdims=True) > 0.5
+    assert not later
+
+    for stream in range(2):
         for chunk in range(CHUNKS):
             bulk_copy(stream, chunk).wait_recv()
         for step in range(STEPS):
             changed_copy(stream, step, STEPS - step).wait_recv()
-        newest = [changed_in[stream, step, STEPS - step - 1] for step in range(STEPS)]
-        newest.append(jnp.zeros((lanes - STEPS * rows, part), bf16))
-        newest = jnp.concatenate(newest, axis=0)
-        for q in range(PARTS):
-            chosen = jnp.where(lax.rem(slot_lane, rows) // CAP == q, spread, 0.0).astype(bf16)
-            newer = jnp.dot(chosen, newest, preferred_element_type=f32)
-            older = bulk_in[stream, :, cols(q)].astype(f32)
-            out[0, :, cols(q)] = jnp.where(seen, newer, older).astype(bf16)
+            newest_out[stream, rows * step : rows * (step + 1)] = changed_in[
+                stream, step, STEPS - step - 1
+            ]
 
     for copy in unsent:
         copy.wait_send()
+
+
+def merge_kernel(fwd_moved, rev_moved, spread_ref, newest_ref, fwd_out, rev_out):
+    q = pl.program_id(0)
+    rows = PARTS * CAP
+    for stream, moved, out in ((0, fwd_moved, fwd_out), (1, rev_moved, rev_out)):
+        spread = spread_ref[stream]
+        seen = jnp.sum(spread, axis=1, keepdims=True) > 0.5
+        slot_lane = lax.broadcasted_iota(jnp.int32, spread.shape, 1)
+        chosen = jnp.where(lax.rem(slot_lane, rows) // CAP == q, spread, 0.0)
+        newer = jnp.dot(
+            chosen.astype(jnp.bfloat16), newest_ref[stream], preferred_element_type=jnp.float32
+        )
+        out[0] = jnp.where(seen, newer, moved[0].astype(jnp.float32)).astype(jnp.bfloat16)
 
 
 def relay_local(
@@ -529,11 +544,16 @@
     vmem = pl.BlockSpec(memory_space=pltpu.VMEM)
     names = routes_fwd.shape[3]
     dma = pltpu.SemaphoreType.DMA
-    return pl.pallas_call(
+    moved = [jax.ShapeDtypeStruct(fwd_state.shape, bf16)] * 2
+    fwd_moved, rev_moved, spread, newest = pl.pallas_call(
         relay_kernel,
-        out_shape=[jax.ShapeDtypeStruct(fwd_state.shape, bf16)] * 2,
+        out_shape=moved
+        + [
+            jax.ShapeDtypeStruct((2, tokens, 128), jnp.float32),
+            jax.ShapeDtypeStruct((2, 128, part), bf16),
+        ],
         in_specs=[in_hbm] * 10,
-        out_specs=[vmem, vmem],
+        out_specs=[in_hbm, in_hbm, vmem, vmem],
         scratch_shapes=[
             pltpu.VMEM((2, tokens, width), bf16),
             pltpu.VMEM((1, width), jnp.float32),
@@ -552,7 +572,6 @@
             pltpu.VMEM((2, STEPS, chips - 1, rows, part), bf16),
             pltpu.VMEM((2, STEPS, rows, part), bf16),
             pltpu.VMEM((2, STEPS, STEPS, rows, part), bf16),
-            pltpu.VMEM((2, tokens, width), bf16),
             dma((10,)),
             dma((3,)),
             dma((3,)),
@@ -584,6 +603,20 @@
         w_down,
         *(x.transpose(0, 1, 3, 2) for x in (routes_fwd, scores_fwd, routes_rev, scores_rev)),
     )
+    block = pl.BlockSpec((1, tokens, part), lambda q: (0, 0, q))
+    return pl.pallas_call(
+        merge_kernel,
+        grid=(PARTS,),
+        out_shape=moved,
+        in_specs=[
+            block,
+            block,
+            pl.BlockSpec(spread.shape, lambda q: (0, 0, 0)),
+            pl.BlockSpec(newest.shape, lambda q: (0, 0, 0)),
+        ],
+        out_specs=[block, block],
+        compiler_params=pltpu.CompilerParams(vmem_limit_bytes=64 * 1024 * 1024),
+    )(fwd_moved, rev_moved, spread, newest)
 
 
 def solution(mesh):

time: 68.2 us -> 69 us (1.012)
  Pallas kernels: 64.7 us -> 68.1 us
  local copies, waits for them, and re-layouts: 2.64 us -> 0 us
    pallas_call x1 -> x2, Pallas kernels: 64.7 us -> 68.1 us  [the longest x1 64.2 us: relay_local(): pl.pallas_call(relay_kernel, out_shape=moved + [jax.ShapeDtypeStruct((2,...]
    unnamed x4 -> x0, local copies, waits for them, and re-layouts: 2.64 us -> none
where the time goes in v5:
time: 69 us; the launch traced here: 68.7 us
  Pallas kernels  68.1 us (99%)
    pallas_call x1, Pallas kernels, relay_local(): pl.pallas_call(relay_kernel, out_shape=moved + [jax.ShapeDtypeStruct((2,...  64.2 us
    pallas_call x1, Pallas kernels, relay_local(): pl.pallas_call(merge_kernel, grid=(PARTS,), out_shape=moved, in_specs=[bl...  3.91 us

profile of v5, /device:TPU:0, one launch (start us, length us, event | category | flops | bytes accessed | tf_op | source)
XLA Modules:
  0.0 68.7 jit_solution(1648149469190412941)
XLA Ops:
  0.6 64.2 %shard_map.113 = (bf16[1,64,3584]{2,1,0:T(8,128)(2,1)}, bf16[1,64,3584]{2,1,0:T(8,128)(2,1)}, f32[2,64,128]{2,1,0:T(8,128)}, bf16[2,128,896]{2,1,0:T(8,128)(2,1)}) custom-call(bf16[1,64,3584]{2,1,0:T(8,128)(2,1)} %fwd_hbm.1, bf16[1,64,3584]{2,1,0:T(8,128)(2,1)} %rev_hbm.1, f32[1,3584]{1,0:T(1,128)} %gain_hbm.1, bf16[1,3584,128]{2,1,0:T(8,128)(2,1)} %gate_hbm.1, ...), custom_call_target="tpu_custom_call" | custom-call | flops 1000000000 | bytes 8000000 | tf_op jit(solution)/shard_map/pallas_call | solution.py:548
  64.8 3.9 %shard_map.114 = (bf16[1,64,3584]{2,1,0:T(8,128)(2,1)}, bf16[1,64,3584]{2,1,0:T(8,128)(2,1)}) custom-call(bf16[1,64,3584]{2,1,0:T(8,128)(2,1)} %get-tuple-element.6.fwd_moved, bf16[1,64,3584]{2,1,0:T(8,128)(2,1)} %get-tuple-element.7.rev_moved, f32[2,64,128]{2,1,0:T(8,128)} %get-tuple-element.8.spread_ref, bf16[2,128,896]{2,1,0:T(8,128)(2,1)} %get-tuple-element.9.newest_ref), custom_call_target="tpu_custom_call" | custom-call | tf_op jit(solution)/shard_map/pallas_call | solution.py:607
